TPU v7x, 256 devices: a whole 4x4x8 slice. The times are simulated.
256 devices in a mesh: rep: 32 (over y, x, core), fsdp: 8 (over z).
Axes of the slice: x: 4, y: 4, z: 8, core: 2. Of those that a mesh axis runs over, the one named last changes fastest.
Arguments:
- codes: bfloat16 [32, 4096, 1024], P('rep', 'fsdp'), may hold values from -127 to 127
- block_scales: float32 [32, 4096, 8], P('rep', 'fsdp'), may hold values from 0.002 to 0.02
- params: bfloat16 [4096, 1024], P('fsdp'), may hold values from -6 to 6
- momentum: bfloat16 [4096, 1024], P('fsdp'), may hold values from -3 to 3
Outputs:
- new_params: bfloat16 [4096, 1024], replicated
- new_momentum: bfloat16 [4096, 1024], P('fsdp')
All inputs are finite; a program needn't handle non-finite values.
Results may differ from a plain program's by a relative error of at most 0.006.
Values may be sent and summed in bfloat16 or wider, within the bound.
A program may use at most 64 MiB of HBM per device.

v0:
```python
import jax
import jax.numpy as jnp
from jax import lax
from jax.sharding import Mesh
from jax.sharding import PartitionSpec as P

REP = ("rep_0", "rep_1", "rep_2")


def filled_up(lines, peers):
    spare = -len(lines) % peers
    return jnp.pad(lines, [(0, spare)] + [(0, 0)] * (lines.ndim - 1))


def sent_to_all(shard, axis):
    copies = jnp.broadcast_to(shard, (lax.axis_size(axis), *shard.shape))
    return lax.all_to_all(copies, axis, split_axis=0, concat_axis=0, tiled=True)


def joined_along(blocks, dim):
    blocks = jnp.moveaxis(blocks, 0, dim)
    lengths = blocks.shape
    return blocks.reshape(*lengths[:dim], lengths[dim] * lengths[dim + 1], *lengths[dim + 2 :])


def whole_of(shard, axes, dim):
    far, near = axes
    first = sent_to_all(shard, far)
    blocks = jnp.swapaxes(sent_to_all(first, near), 0, 1)
    return joined_along(blocks.reshape(-1, *shard.shape), dim)


def in_blocks(shard, dim, peers):
    before, after = (shard.shape[:dim], shard.shape[dim + 1 :])
    return jnp.moveaxis(shard.reshape(*before, peers, -1, *after), dim, 0)


def sum_at_owner(shard, axis, dim):
    blocks = in_blocks(shard, dim, lax.axis_size(axis))
    arrived = lax.all_to_all(blocks, axis, split_axis=0, concat_axis=0, tiled=True)
    return arrived.astype(jnp.float32).sum(axis=0)


def summed_rows(shard, axes, dim):
    far, near = axes
    own = sum_at_owner(in_blocks(shard, dim, lax.axis_size(far)), near, dim + 1)
    return jnp.sum(
        lax.all_to_all(own.astype(jnp.bfloat16), far, 0, 0, tiled=True).astype(jnp.float32), axis=0
    )


def sum_by_parts(shard, axes):
    lines = shard.reshape(-1, shard.shape[-1])
    padded = filled_up(lines, lax.axis_size(axes[0]) * lax.axis_size(axes[1]))
    whole = whole_of(summed_rows(padded, axes, 0).astype(jnp.bfloat16), axes, 0)
    return lax.slice_in_dim(whole, 0, len(lines)).reshape(shard.shape).astype(jnp.float32)


def dequantize(code_rows, scale_rows):
    count, width = code_rows.shape
    pieces = (
        code_rows.astype(jnp.float32).reshape(count, width // 128, 128) * scale_rows[:, :, None]
    )
    return pieces.reshape(count, width)


def outer_update(total, params, momentum, replicas):
    delta = total / replicas
    moment = 0.9 * momentum.astype(jnp.float32) + delta
    updated = (params.astype(jnp.float32) - 0.7 * (delta + 0.9 * moment)).astype(jnp.bfloat16)
    return (updated, moment.astype(jnp.bfloat16))


def local(codes, block_scales, params, momentum):
    replicas = lax.axis_size(REP)
    local_term = dequantize(codes[0], block_scales[0])
    total = sum_by_parts(local_term.astype(jnp.bfloat16), (("rep_0", "rep_1"), "rep_2"))
    updated, new_momentum = outer_update(total, params, momentum, replicas)
    new_params = lax.all_gather(updated, "fsdp", axis=0, tiled=True)
    return (new_params, new_momentum)


def solution(mesh):
    finer = Mesh(
        mesh.devices.reshape(4, 4, 2, mesh.shape["fsdp"]), ("rep_0", "rep_1", "rep_2", "fsdp")
    )
    placed = (P(REP, "fsdp", None), P(REP, "fsdp", None), P("fsdp", None), P("fsdp", None))
    return jax.shard_map(
        local, mesh=finer, in_specs=placed, out_specs=(P(), P("fsdp", None)), check_vma=False
    )
```

profile of v0, /device:TPU:1, one launch (start us, length us, event | category | flops | bytes accessed | tf_op | source)
XLA Modules:
  0.0 167.0 jit_solution(15279222004547587232)
XLA Ops:
  7.2 0.0 all-gather.2.cloned.1.call-start
  7.2 0.8 copy.11
  8.1 0.6 mul.27
  8.7 0.0 copy-start
  8.7 1.5 mul.28
  10.2 0.0 copy-done
  10.2 1.9 %fusion.5 = bf16[2,16,16,1024]{3,2,0,1:T(8,128)(2,1)S(1)} fusion(f32[16,2,16,1024]{3,2,1,0:T(8,128)} %mul.28, bf16[16,2,16,1024]{3,2,1,0:T(8,128)(2,1)S(1)} %bitcast.20), kind=kLoop, calls=%fused_computation.9 | loop fusion | flops 1572864 | bytes 4194304 | tf_op jit(solution)/shard_map/transpose | solution.py:35
  12.1 0.1 copy.12
  12.2 7.4 %all_to_all.20 = bf16[2,16,16,1024]{3,2,1,0:T(8,128)(2,1)S(1)} all-to-all(bf16[2,16,16,1024]{3,2,1,0:T(8,128)(2,1)S(1)} %copy.12), channel_id=1, replica_groups=mesh['rep_0'=4,'rep_1'=4,'rep_2'=2,'fsdp'=8] {'rep_2'}, dimensions={0} | all-to-all | bytes 2097152 | tf_op jit(solution)/shard_map/all_to_all | solution.py:40
  19.6 0.3 reduce_sum.24
  19.9 15.5 %all_to_all.21 = bf16[16,16,1024]{2,1,0:T(8,128)(2,1)S(1)} all-to-all(bf16[16,16,1024]{2,1,0:T(8,128)(2,1)S(1)} %reduce_sum.24), channel_id=1, replica_groups=mesh['rep_0'=4,'rep_1'=4,'rep_2'=2,'fsdp'=8] {'rep_0','rep_1'}, dimensions={0} | all-to-all | bytes 1048576 | tf_op jit(solution)/shard_map/all_to_all | solution.py:48
  35.4 0.1 reduce_sum.25
  35.5 0.1 broadcast_in_dim.6
  35.6 13.4 %all_to_all.22 = bf16[16,16,1024]{2,1,0:T(8,128)(2,1)S(1)} all-to-all(bf16[16,16,1024]{2,1,0:T(8,128)(2,1)S(1)} %broadcast_in_dim.6), channel_id=1, replica_groups=mesh['rep_0'=4,'rep_1'=4,'rep_2'=2,'fsdp'=8] {'rep_0','rep_1'}, dimensions={0} | all-to-all | bytes 1048576 | tf_op jit(solution)/shard_map/all_to_all | solution.py:17
  49.0 0.1 broadcast_in_dim.7
  49.1 6.5 %all_to_all.23 = bf16[2,16,16,1024]{3,2,1,0:T(8,128)(2,1)S(1)} all-to-all(bf16[2,16,16,1024]{3,2,1,0:T(8,128)(2,1)S(1)} %broadcast_in_dim.7), channel_id=1, replica_groups=mesh['rep_0'=4,'rep_1'=4,'rep_2'=2,'fsdp'=8] {'rep_2'}, dimensions={0} | all-to-all | bytes 2097152 | tf_op jit(solution)/shard_map/all_to_all | solution.py:17
  55.7 0.0 copy-start.1
  55.7 0.0 copy-start.2
  55.7 0.3 convert_multiply_fusion.1
  55.9 1.0 copy-done.1
  56.9 0.3 copy-done.2
  57.2 2.0 %fusion.4 = (bf16[512,1024]{1,0:T(8,128)(2,1)}, bf16[512,1024]{1,0:T(8,128)(2,1)}) fusion(f32[2,16,16,1024]{3,2,0,1:T(8,128)S(1)} %convert_multiply_fusion.1, bf16[512,1024]{1,0:T(8,128)(2,1)S(1)} %copy-done.1, bf16[512,1024]{1,0:T(8,128)(2,1)S(1)} %copy-done.2), kind=kLoop, calls=%fused_computation.7 | loop fusion | flops 5242880 | bytes 6291456 | tf_op jit(solution)/shard_map/convert_element_type | solution.py:71
  59.3 0.0 all-gather.2.cloned.1.call-update
  59.3 93.1 %all-gather.2.cloned.1.call-done = bf16[4096,1024]{1,0:T(8,128)(2,1)} async-done(((bf16[512,1024]{1,0:T(8,128)(2,1)}), bf16[4096,1024]{1,0:T(8,128)(2,1)}) %all-gather.2.cloned.1.call-update) | async-done | bytes 8388624 | tf_op jit(solution)/shard_map/all_gather | solution.py:79
  152.4 7.8 %copy.16 = bf16[4096,1024]{1,0:T(8,128)(2,1)} copy(bf16[4096,1024]{1,0:T(8,128)(2,1)} %all-gather.2.cloned.1.call-done) | data formatting | bytes 16777216
Async XLA Ops:
  7.2 145.2 %all-gather.2.cloned.1.call-start = ((), (), s32[]{:S(2)}) async-start(), calls=%async_computation.4 | async-start | bytes 9437184 | tf_op jit(solution)/shard_map/all_gather | solution.py:79
  8.7 1.5 copy-start
  55.7 1.2 copy-start.1
  55.7 1.5 copy-start.2
Sparse Core Ops, SparseCore 0:
  59.4 92.9 all-gather.1
where the time goes:
time: 167 us
  waiting for transfers between devices  93.1 us (56%)
  blocking collectives  42.9 us (26%)
  between operations  14.1 us (8%)
  local copies, waits for them, and re-layouts  12.2 us (7%)
  other arithmetic  4.57 us (3%)
    all_gather x1, waiting for transfers between devices, local(): new_params = lax.all_gather(updated, 'fsdp', axis=0, tiled=True)  93.1 us
    all_to_all x2, blocking collectives, sent_to_all(): return lax.all_to_all(copies, axis, split_axis=0, concat_axis=0, tiled=True)  20 us
    all_to_all x1, blocking collectives, summed_rows(): lax.all_to_all(own.astype(jnp.bfloat16), far, 0, 0, tiled=True)  15.5 us
    unnamed x7, local copies, waits for them, and re-layouts  9.05 us
    all_to_all x1, blocking collectives, sum_at_owner(): lax.all_to_all(blocks, axis, split_axis=0, concat_axis=0, tiled=True)  7.44 us
  transfers between devices with their start and end apart: 1, of which 1 were waited for; matrix products, arithmetic and copies ran while one was open for 0% of the time, Pallas kernels for 0%

commit v1 on v0

--- a/solution.py
+++ b/solution.py
@@ -1,3 +1,4 @@
+import functools
 import jax
 import jax.numpy as jnp
 from jax import lax
@@ -5,6 +6,14 @@
 from jax.sharding import PartitionSpec as P
 
 REP = ("rep_0", "rep_1", "rep_2")
+
+
+def prepare_ranges(local_x, mesh_name):
+    outer = jnp.concatenate(lax.axis_size(mesh_name) * [local_x], axis=0)
+    return lax.all_to_all(outer, mesh_name, 0, 0, tiled=True)
+
+
+_watch_hubs = functools.partial(prepare_ranges, mesh_name="fsdp")
 
 
 def filled_up(lines, peers):
@@ -76,7 +85,7 @@
     local_term = dequantize(codes[0], block_scales[0])
     total = sum_by_parts(local_term.astype(jnp.bfloat16), (("rep_0", "rep_1"), "rep_2"))
     updated, new_momentum = outer_update(total, params, momentum, replicas)
-    new_params = lax.all_gather(updated, "fsdp", axis=0, tiled=True)
+    new_params = _watch_hubs(updated)
     return (new_params, new_momentum)
 
 

time: 167 us -> 254 us (1.52)
  blocking collectives: 42.9 us -> 237 us
  waiting for transfers between devices: 93.1 us -> 0 us
  between operations: 14.1 us -> 0.77 us
    all_to_all x0 -> x1, blocking collectives: none -> 193 us  [prepare_ranges(): return lax.all_to_all(outer, mesh_name, 0, 0, tiled=True)]
    all_gather x1 -> x0, waiting for transfers between devices: 93.1 us -> none  [local(): new_params = lax.all_gather(updated, 'fsdp', axis=0, tiled=True)]
    unnamed x7 -> x12, local copies, waits for them, and re-layouts: 9.05 us -> 8.26 us
  transfers between devices with their start and end apart: 1 -> 0, of which waited for: 1 -> 0; matrix products, arithmetic and copies ran while one was open for 0% -> 0% of each run, Pallas kernels for 0% -> 0%
where the time goes in v1:
time: 254 us; the launch traced here: 253 us
  blocking collectives  237 us (93%)
  local copies, waits for them, and re-layouts  11.5 us (5%)
  other arithmetic  4.49 us (2%)
    all_to_all x1, blocking collectives, prepare_ranges(): return lax.all_to_all(outer, mesh_name, 0, 0, tiled=True)  193 us
    all_to_all x2, blocking collectives, sent_to_all(): return lax.all_to_all(copies, axis, split_axis=0, concat_axis=0, tiled=True)  20.1 us
    all_to_all x1, blocking collectives, summed_rows(): lax.all_to_all(own.astype(jnp.bfloat16), far, 0, 0, tiled=True)  15.5 us
    unnamed x12, local copies, waits for them, and re-layouts  8.26 us
    all_to_all x1, blocking collectives, sum_at_owner(): lax.all_to_all(blocks, axis, split_axis=0, concat_axis=0, tiled=True)  7.57 us

profile of v1, /device:TPU:1, one launch (start us, length us, event | category | flops | bytes accessed | tf_op | source)
XLA Modules:
  0.0 253.3 jit_solution(172869467467009527)
XLA Ops:
  0.6 0.8 copy.11
  1.5 0.6 mul.27
  2.1 1.5 mul.28
  3.6 2.2 fusion.5
  5.8 0.0 copy-start
  5.8 0.1 copy.12
  5.9 7.6 %all_to_all.32 = bf16[2,16,16,1024]{3,2,1,0:T(8,128)(2,1)S(1)} all-to-all(bf16[2,16,16,1024]{3,2,1,0:T(8,128)(2,1)S(1)} %copy.12), channel_id=1, replica_groups=mesh['rep_0'=4,'rep_1'=4,'rep_2'=2,'fsdp'=8] {'rep_2'}, dimensions={0} | all-to-all | bytes 2097152 | tf_op jit(solution)/shard_map/all_to_all | solution.py:49
  13.4 0.3 reduce_sum.24
  13.7 15.5 %all_to_all.33 = bf16[16,16,1024]{2,1,0:T(8,128)(2,1)S(1)} all-to-all(bf16[16,16,1024]{2,1,0:T(8,128)(2,1)S(1)} %reduce_sum.24), channel_id=1, replica_groups=mesh['rep_0'=4,'rep_1'=4,'rep_2'=2,'fsdp'=8] {'rep_0','rep_1'}, dimensions={0} | all-to-all | bytes 1048576 | tf_op jit(solution)/shard_map/all_to_all | solution.py:57
  29.2 0.0 copy-start.1
  29.2 0.1 reduce_sum.25
  29.3 0.1 broadcast_in_dim.6
  29.4 13.6 %all_to_all.34 = bf16[16,16,1024]{2,1,0:T(8,128)(2,1)S(1)} all-to-all(bf16[16,16,1024]{2,1,0:T(8,128)(2,1)S(1)} %broadcast_in_dim.6), channel_id=1, replica_groups=mesh['rep_0'=4,'rep_1'=4,'rep_2'=2,'fsdp'=8] {'rep_0','rep_1'}, dimensions={0} | all-to-all | bytes 1048576 | tf_op jit(solution)/shard_map/all_to_all | solution.py:26
  42.9 0.1 broadcast_in_dim.7
  43.1 6.5 %all_to_all.35 = bf16[2,16,16,1024]{3,2,1,0:T(8,128)(2,1)S(1)} all-to-all(bf16[2,16,16,1024]{3,2,1,0:T(8,128)(2,1)S(1)} %broadcast_in_dim.7), channel_id=1, replica_groups=mesh['rep_0'=4,'rep_1'=4,'rep_2'=2,'fsdp'=8] {'rep_2'}, dimensions={0} | all-to-all | bytes 2097152 | tf_op jit(solution)/shard_map/all_to_all | solution.py:26
  49.6 0.3 convert_multiply_fusion.1
  49.9 0.0 copy-done
  49.9 0.0 copy-done.1
  49.9 1.7 fusion.4
  51.6 0.1 constant_dynamic-update-slice_fusion.7
  51.7 0.1 constant_dynamic-update-slice_fusion.6
  51.7 0.1 constant_dynamic-update-slice_fusion.5
  51.8 0.1 constant_dynamic-update-slice_fusion.4
  51.9 0.1 constant_dynamic-update-slice_fusion.3
  52.0 0.1 constant_dynamic-update-slice_fusion.2
  52.1 0.1 constant_dynamic-update-slice_fusion.1
  52.1 0.1 constant_dynamic-update-slice_fusion
  52.2 193.3 %all_to_all.36 = bf16[8,512,1024]{2,1,0:T(8,128)(2,1)} all-to-all(bf16[8,512,1024]{2,1,0:T(8,128)(2,1)S(1)} %bitcast.23), channel_id=1, replica_groups=mesh['rep_0'=4,'rep_1'=4,'rep_2'=2,'fsdp'=8] {'fsdp'}, dimensions={0} | all-to-all | bytes 16777216 | tf_op jit(solution)/shard_map/all_to_all | solution.py:13
  245.5 7.8 %copy.23 = bf16[4096,1024]{1,0:T(8,128)(2,1)} copy(bf16[4096,1024]{1,0:T(8,128)(2,1)} %bitcast.22) | data formatting | bytes 16777216
Async XLA Ops:
  5.8 44.1 %copy-start = (bf16[512,1024]{1,0:T(8,128)(2,1)S(1)}, bf16[512,1024]{1,0:T(8,128)(2,1)}, u32[]{:S(2)}) copy-start(bf16[512,1024]{1,0:T(8,128)(2,1)} %param.7) | copy-start | bytes 3145732
  29.2 20.6 %copy-start.1 = (bf16[512,1024]{1,0:T(8,128)(2,1)S(1)}, bf16[512,1024]{1,0:T(8,128)(2,1)}, u32[]{:S(2)}) copy-start(bf16[512,1024]{1,0:T(8,128)(2,1)} %param.6) | copy-start | bytes 3145732
